TPU v7x, 32 devices: a whole 2x2x4 slice. The times are simulated.
32 devices in a mesh: dec: 16 (over z, y, x), tp: 2 (over core).
Axes of the slice: x: 2, y: 2, z: 4, core: 2. Of those that a mesh axis runs over, the one named last changes fastest.
Arguments:
- queries: bfloat16 [4, 128, 8192], P(None, 'dec', 'tp'), may hold values from -600 to 600
- new_kv: bfloat16 [4, 128, 2, 512], P(None, 'dec', None, 'tp'), may hold values from -6 to 6
- kv_pool: bfloat16 [1024, 32, 2, 512], P('dec', None, None, 'tp'), may hold values from -6 to 6
- block_table: int32 [128, 8], P('dec'), may hold values from 0 to 63, as said below
- lengths: int32 [128], P('dec'), may hold values from 1 to 252, as said below
- new_group: int32 [128], P('dec'), may hold values from 0 to 15, as said below
- hidden_rows: bfloat16 [4, 128, 4096], P(None, 'dec', 'tp'), may hold values from -6 to 6
- norm_gain: bfloat16 [4096], replicated, may hold values from 0.099609375 to 1.8984375
- routes: int32 [4, 128, 8], P(None, 'dec'), may hold values from 0 to 15, all different within a row; in each aligned block of 8 rows (0 to 7, 8 to 15, ..., all dimensions but the last counted through in order) at most 8 rows name the same one
- route_logits: float32 [4, 128, 8], P(None, 'dec'), may hold values from -2 to 301
- w_gate: bfloat16 [16, 4096, 1536], P('dec', None, 'tp'), may hold values from -0.09375 to 0.09375
- w_up: bfloat16 [16, 4096, 1536], P('dec', None, 'tp'), may hold values from -0.09375 to 0.09375
- w_down: bfloat16 [16, 1536, 4096], P('dec', 'tp'), may hold values from -0.15625 to 0.15625
Outputs:
- attn_out: bfloat16 [4, 128, 8192], P(None, 'dec', 'tp')
- moe_out: bfloat16 [4, 128, 4096], P(None, 'dec', 'tp')
- pool_after: bfloat16 [1024, 32, 2, 512], P('dec', None, None, 'tp')
Inputs may be any that keep to these rules, and one draw needn't show every extreme that they name: `block_table`: within each group's 8 requests the table is a permutation of the group's 8 * 8 blocks. `lengths`: each group has a request of 252 tokens. `new_group`: in each group exactly one request names another group, all others name their own; the moves form one cycle through all groups, so each group receives exactly one request. `routes`: A request's 8 experts at a step are distinct; in one step the requests of one group name no expert more than 8 times.
All inputs are finite; a program needn't handle non-finite values.
Results may differ from a plain program's by a relative error of at most 0.0071.
Values may be sent and summed in bfloat16 or wider, within the bound.
A program may use at most 128 MiB of HBM per device.

v0:
```python
import math

import jax
import jax.numpy as jnp
from jax import lax
from jax.experimental import pallas as pl
from jax.experimental.pallas import tpu as pltpu
from jax.sharding import PartitionSpec as P

HD = 128


eps_norm = 1e-06


def rms_scaled(values, gain_vec):
    widened = values.astype(jnp.float32)
    factor = lax.rsqrt(jnp.mean(widened * widened, axis=-1, keepdims=True) + eps_norm)
    return (widened * factor * gain_vec.astype(jnp.float32)).astype(jnp.bfloat16)


def attend_step(query_rows, keys_all, values_all, lengths, step_index):
    row_count, cache_span, kv_local, head_dim = keys_all.shape
    group_ratio = query_rows.shape[1] // (kv_local * head_dim)
    grouped = query_rows.reshape(row_count, kv_local, group_ratio, head_dim)
    scores = jnp.einsum("rkgd,rlkd->rkgl", grouped, keys_all, preferred_element_type=jnp.float32)
    scores = scores * (1.0 / math.sqrt(head_dim))
    visible = jnp.arange(cache_span)[None, :] < (lengths + step_index + 1)[:, None]
    visible = visible[:, None, None, :]
    masked = jnp.where(visible, scores, -1e30)
    highest = jnp.max(masked, axis=-1, keepdims=True)
    weights = jnp.where(visible, jnp.exp(masked - highest), 0.0)
    weight_sum = jnp.sum(weights, axis=-1, keepdims=True)
    shares = (weights / weight_sum).astype(jnp.bfloat16)
    mixed_out = jnp.einsum(
        "rkgl,rlkd->rkgd", shares, values_all, preferred_element_type=jnp.float32
    )
    return mixed_out.astype(jnp.bfloat16).reshape(row_count, -1)


def slot_layout(route_ids, experts_all, capacity):
    flat_ids = route_ids.reshape(-1)
    hits_table = (flat_ids[:, None] == jnp.arange(experts_all)[None, :]).astype(jnp.int32)
    earlier = jnp.cumsum(hits_table, axis=0) - hits_table
    placing = jnp.sum(earlier * hits_table, axis=1)
    return flat_ids * capacity + placing


def expert_apply(normed, w_gate, w_up, w_down):
    flat_rows = normed.reshape(-1, normed.shape[-1])
    gate_out = jnp.dot(flat_rows, w_gate[0], preferred_element_type=jnp.float32)
    up_out = jnp.dot(flat_rows, w_up[0], preferred_element_type=jnp.float32)
    inner_act = (jax.nn.silu(gate_out) * up_out).astype(jnp.bfloat16)
    partial_value = jnp.dot(inner_act, w_down[0], preferred_element_type=jnp.float32)
    partial_value = partial_value.reshape(normed.shape[0], normed.shape[1], -1)
    summed = lax.psum_scatter(partial_value, "tp", scatter_dimension=2, tiled=True).astype(
        jnp.bfloat16
    )
    return lax.all_to_all(summed, "dec", split_axis=0, concat_axis=0, tiled=True)


def body_general(
    queries,
    new_kv,
    kv_pool,
    block_table,
    lengths,
    new_group,
    hidden_rows,
    norm_gain,
    routes,
    route_logits,
    w_gate,
    w_up,
    w_down,
):
    step_total = new_kv.shape[0]
    req_local = new_kv.shape[1]
    kv_width = new_kv.shape[3]
    block_local = kv_pool.shape[0]
    block_tokens = kv_pool.shape[1]
    blocks_per = block_table.shape[1]
    span_total = blocks_per * block_tokens
    kv_local = kv_width // HD
    request_ids = jnp.arange(req_local)
    flat_pool = kv_pool.reshape(block_local * block_tokens, 2, kv_width)
    for step_index in range(step_total):
        position = lengths + step_index
        target_rows = (
            block_table[request_ids, position // block_tokens] * block_tokens
            + position % block_tokens
        )
        flat_pool = flat_pool.at[target_rows].set(new_kv[step_index])
    pool_now = flat_pool.reshape(block_local, block_tokens, 2, kv_width)
    cached = pool_now[block_table].reshape(req_local, span_total, 2, kv_local, HD)
    keys_all = cached[:, :, 0]
    values_all = cached[:, :, 1]
    attn_out = jnp.stack(
        [
            attend_step(queries[step_index], keys_all, values_all, lengths, step_index)
            for step_index in range(step_total)
        ]
    )
    group_self = lax.axis_index("dec")
    group_count = lax.axis_size("dec")
    leaving = (new_group != group_self).astype(jnp.int32)
    depart_slot = jnp.argmax(leaving)
    destination = new_group[depart_slot]
    depart_blocks = block_table[depart_slot]
    outgoing = pool_now[depart_blocks].reshape(span_total, 2, kv_width)
    every_cache, every_dest = (
        lax.all_gather(outgoing[None], "dec", axis=0, tiled=True),
        lax.all_gather(destination.reshape(1), "dec", axis=0, tiled=True),
    )
    source = jnp.argmax((every_dest == group_self).astype(jnp.int32))
    incoming = lax.dynamic_index_in_dim(every_cache, source, 0, keepdims=False)
    pool_after = pool_now.at[depart_blocks].set(
        incoming.reshape(blocks_per, block_tokens, 2, kv_width)
    )
    top_count = routes.shape[2]
    capacity = min(req_local, 2 * ((req_local * top_count + group_count - 1) // group_count))
    owners = jnp.repeat(request_ids, top_count)
    moe_list = []
    for step_index in range(step_total):
        slot_index = slot_layout(routes[step_index], group_count, capacity)
        route_probs = jax.nn.softmax(route_logits[step_index], axis=-1)
        local_rows = hidden_rows[step_index]
        buffer = (
            jnp.zeros((group_count * capacity, local_rows.shape[1]), jnp.bfloat16)
            .at[slot_index]
            .set(local_rows[owners])
        )
        full_rows = lax.all_gather(
            lax.all_to_all(
                buffer.reshape(group_count, capacity, -1),
                "dec",
                split_axis=0,
                concat_axis=0,
                tiled=True,
            ),
            "tp",
            axis=2,
            tiled=True,
        )
        returned_rows = expert_apply(rms_scaled(full_rows, norm_gain), w_gate, w_up, w_down)
        picked = returned_rows.reshape(group_count * capacity, -1)[slot_index].astype(jnp.float32)
        weighted = picked * route_probs.reshape(-1, 1)
        moe_list.append(
            jnp.sum(weighted.reshape(req_local, top_count, -1), axis=1).astype(jnp.bfloat16)
        )
    moe_out = jnp.stack(moe_list)
    return (attn_out, moe_out, pool_after)


MESH = pl.DeviceIdType.MESH
F32 = jnp.float32
BF = jnp.bfloat16
SS, ZG, X1, Y1, X2, Y2, SIB, TP, RA, RB, RA2, RB2, RZ = range(13)
PIECE = 16


def exchange_kernel(
    hid, gain, routes, logits, out_cache, wg_hbm, wu_hbm, wd_hbm,
    moe_ref, inc_ref,
    wg, wu, wd, gath, ss_out, ss_in, act, acc, tp_out, tp_in,
    a_out, a_in, b_out, b_in, a2_out, a2_in, b2_out, b2_in, z_out, z_in,
    mig_in, mig_out, wsem, ssem, rsem, m_s1, m_r1, m_s2, m_r2, local_sem,
):
    me = lax.axis_index("dec")
    core = lax.axis_index("tp")
    x, y, z = me % 2, (me // 2) % 2, me // 4
    x_peer = me + 1 - 2 * x
    y_peer = me + 2 - 4 * y
    z_peers = [me, me + 4 - 8 * (z % 2), ((z + 2) % 4) * 4 + me % 4, (3 - z) * 4 + me % 4]
    half = hid.shape[2]
    quarter = half // 2
    count = 16

    barrier = pltpu.get_barrier_semaphore()
    for m in range(1, count):
        pl.semaphore_signal(barrier, inc=1, device_id={"dec": (me + m) % count}, device_id_type=MESH)
    pl.semaphore_signal(barrier, inc=1, device_id={"tp": 1 - core}, device_id_type=MESH)

    weights = [
        pltpu.make_async_copy(src.at[0], dst, wsem.at[i])
        for i, (src, dst) in enumerate(((wg_hbm, wg), (wu_hbm, wu), (wd_hbm, wd)))
    ]
    for copy in weights:
        copy.start()

    raw = jnp.concatenate([hid[t].astype(F32) for t in range(hid.shape[0])], axis=0)
    own_sum = jnp.sum(raw * raw, axis=-1, keepdims=True)
    ss_out[...] = jnp.broadcast_to(own_sum, ss_out.shape)
    pl.semaphore_wait(barrier, count)

    def remote(kind, q, src, dst, peer):
        return pltpu.make_async_remote_copy(
            src_ref=src, dst_ref=dst, send_sem=ssem.at[kind, q], recv_sem=rsem.at[kind, q],
            device_id=peer, device_id_type=MESH,
        )

    ss_copy = remote(SS, 0, ss_out, ss_in, {"tp": 1 - core})
    ss_copy.start()

    lane = lax.broadcasted_iota(jnp.int32, (raw.shape[0], 128), 1)
    logit = jnp.concatenate([logits[t] for t in range(hid.shape[0])], axis=0)
    route = jnp.concatenate([routes[t] for t in range(hid.shape[0])], axis=0)
    grown = jnp.exp(logit - jnp.max(logit, axis=-1, keepdims=True))
    prob = grown / jnp.sum(grown, axis=-1, keepdims=True)
    dense = jnp.zeros(lane.shape, F32)
    for k in range(route.shape[1]):
        hit = (lane % 16) == route[:, k : k + 1]
        dense = dense + jnp.where(hit, prob[:, k : k + 1], 0.0)
    high = dense.astype(BF)
    low = (dense - high.astype(F32)).astype(BF)
    packed = jnp.where(lane < 16, high.astype(F32), low.astype(F32)).astype(BF)

    ss_copy.wait()
    total = own_sum + ss_in[:, 0:1]
    factor = lax.rsqrt(total * (1.0 / (2 * half)) + eps_norm)
    own_gain = jnp.where(core == 0, gain[0:1], gain[1:2])
    rows = raw.shape[0]
    gath[core, 0, 0:rows, 0:half] = (raw * factor * own_gain).astype(BF)
    gath[core, 0, 0:rows, half:] = packed

    def slot(q, j, lo=0, hi=None):
        return gath.at[core, q, pl.ds(j * rows, rows), pl.ds(lo, (hi or gath.shape[3]) - lo)]

    sends = []

    def go(copy):
        copy.start()
        sends.append(copy)
        return copy

    x1, y1 = {}, {}

    def spread(q):
        x1[q] = go(remote(X1, q, slot(q, 0), slot(q, 1), {"dec": x_peer}))
        y1[q] = go(remote(Y1, q, slot(q, 0), slot(q, 2), {"dec": y_peer}))

    spread(0)
    zg = {q: go(remote(ZG, q, slot(0, 0), slot(q, 0), {"dec": z_peers[q]})) for q in (1, 2, 3)}

    first = []
    for m in range(1, count):
        peer = (me + m) % count
        copy = pltpu.make_async_remote_copy(
            src_ref=out_cache.at[pl.ds(peer * PIECE, PIECE)], dst_ref=mig_in.at[m],
            send_sem=m_s1.at[m], recv_sem=m_r1.at[m], device_id={"dec": peer}, device_id_type=MESH,
        )
        copy.start()
        first.append(copy)
    mig_in[0] = out_cache[pl.ds(me * PIECE, PIECE)]

    def gather(q):
        if q < 3:
            zg[q + 1].wait_recv()
            spread(q + 1)
        y1[q].wait_recv()
        x2 = go(remote(X2, q, slot(q, 2, 0, quarter), slot(q, 3, 0, quarter), {"dec": x_peer}))
        x1[q].wait_recv()
        y2 = go(remote(Y2, q, slot(q, 1, quarter), slot(q, 3, quarter), {"dec": y_peer}))
        x2.wait_recv()
        y2.wait_recv()
        return go(remote(SIB, q, gath.at[core, q], gath.at[core, q], {"tp": 1 - core}))

    def apply(q):
        if q == 0:
            weights[0].wait()
            weights[1].wait()

        @pl.loop(0, act.shape[1] // 256)
        def _(i):
            cols = pl.ds(pl.multiple_of(i * 256, 256), 256)

            def product(w):
                return jnp.dot(
                    gath[0, q, :, 0:half], w[0:half, cols], preferred_element_type=F32
                ) + jnp.dot(
                    gath[1, q, :, 0:half], w[half : 2 * half, cols], preferred_element_type=F32
                )

            g = product(wg)
            act[:, cols] = (g / (1.0 + jnp.exp(-g)) * product(wu)).astype(BF)

        if q == 0:
            weights[2].wait()
        probs = gath[0, q, :, half:].astype(F32)
        lanes = lax.broadcasted_iota(jnp.int32, probs.shape, 1)
        mine = (lanes == me) | (lanes == me + 16)
        weight = jnp.sum(jnp.where(mine, probs, 0.0), axis=-1, keepdims=True)
        step = 512

        @pl.loop(0, half // step)
        def _(i):
            to = pl.ds(pl.multiple_of(i * step, step), step)
            cols = pl.ds(pl.multiple_of((1 - core) * half + i * step, step), step)
            tp_out[q, :, to] = (
                jnp.dot(act[...], wd[:, cols], preferred_element_type=F32) * weight
            ).astype(BF)

        copy = go(remote(TP, q, tp_out.at[q], tp_in.at[q], {"tp": 1 - core}))

        @pl.loop(0, half // step)
        def _(i):
            to = pl.ds(pl.multiple_of(i * step, step), step)
            cols = pl.ds(pl.multiple_of(core * half + i * step, step), step)
            acc[q, :, to] = jnp.dot(act[...], wd[:, cols], preferred_element_type=F32) * weight

        return copy

    ra, rb, ra2, rb2, rz = {}, {}, {}, {}, {}
    r = rows

    def fold1(q, copy):
        copy.wait_recv()
        acc[q] = acc[q] + tp_in[q].astype(F32)
        a_out[q, 0:r] = acc[q, r : 2 * r, 0:quarter].astype(BF)
        a_out[q, r : 2 * r] = acc[q, 3 * r : 4 * r, 0:quarter].astype(BF)
        ra[q] = go(remote(RA, q, a_out.at[q], a_in.at[q], {"dec": x_peer}))
        b_out[q] = acc[q, 2 * r : 4 * r, quarter:].astype(BF)
        rb[q] = go(remote(RB, q, b_out.at[q], b_in.at[q], {"dec": y_peer}))

    def fold2(q):
        ra[q].wait_recv()
        a2_out[q] = (acc[q, 2 * r : 3 * r, 0:quarter] + a_in[q, r : 2 * r].astype(F32)).astype(BF)
        ra2[q] = go(remote(RA2, q, a2_out.at[q], a2_in.at[q], {"dec": y_peer}))
        rb[q].wait_recv()
        b2_out[q] = (acc[q, r : 2 * r, quarter:] + b_in[q, r : 2 * r].astype(F32)).astype(BF)
        rb2[q] = go(remote(RB2, q, b2_out.at[q], b2_in.at[q], {"dec": x_peer}))
        acc[q, 0:r, 0:quarter] = acc[q, 0:r, 0:quarter] + a_in[q, 0:r].astype(F32)
        acc[q, 0:r, quarter:] = acc[q, 0:r, quarter:] + b_in[q, 0:r].astype(F32)

    def fold3(q):
        ra2[q].wait_recv()
        rb2[q].wait_recv()
        acc[q, 0:r, 0:quarter] = acc[q, 0:r, 0:quarter] + a2_in[q].astype(F32)
        acc[q, 0:r, quarter:] = acc[q, 0:r, quarter:] + b2_in[q].astype(F32)
        if q:
            z_out[q] = acc[q, 0:r].astype(BF)
            rz[q] = go(remote(RZ, q, z_out.at[q], z_in.at[q], {"dec": z_peers[q]}))

    sib = gather(0)
    for copy in first:
        copy.wait()
    width = mig_out.shape[2]
    second = []
    for m in range(count):
        peer = (me + m) % count
        wanted = peer.astype(F32)
        chosen = jnp.zeros((PIECE, width), F32)
        for n in range(count):
            head = mig_in[n, :, width : width + 1].astype(F32)
            chosen = jnp.where(head == wanted, mig_in[n, :, 0:width].astype(F32), chosen)
        mig_out[m] = chosen.astype(BF)
        where = inc_ref.at[pl.ds(me * PIECE, PIECE)]
        if m:
            copy = pltpu.make_async_remote_copy(
                src_ref=mig_out.at[m], dst_ref=where, send_sem=m_s2.at[m], recv_sem=m_r2.at[m],
                device_id={"dec": peer}, device_id_type=MESH,
            )
        else:
            copy = pltpu.make_async_copy(mig_out.at[m], where, local_sem)
        copy.start()
        second.append(copy)

    sib.wait_recv()
    tp0 = apply(0)
    sib = gather(1)
    fold1(0, tp0)
    sib.wait_recv()
    tp1 = apply(1)
    fold2(0)
    sib = gather(2)
    fold1(1, tp1)
    fold3(0)
    sib.wait_recv()
    tp2 = apply(2)
    fold2(1)
    sib = gather(3)
    fold1(2, tp2)
    fold3(1)
    sib.wait_recv()
    tp3 = apply(3)
    fold2(2)
    fold1(3, tp3)
    fold3(2)
    fold2(3)
    for copy in second:
        copy.wait()
    fold3(3)
    result = acc[0, 0:r]
    for q in (1, 2, 3):
        rz[q].wait_recv()
        result = result + z_in[q].astype(F32)
    for t in range(moe_ref.shape[0]):
        moe_ref[t] = result[t * 8 : t * 8 + 8].astype(BF)
    for copy in sends:
        copy.wait_send()


def exchange(hidden, gain, routes, logits, out_cache, w_gate, w_up, w_down):
    steps, req, half = hidden.shape
    rows = steps * req
    quarter = half // 2
    wide = w_gate.shape[2]
    vm = pltpu.VMEM
    scratch = [
        vm(w_gate.shape[1:], BF), vm(w_up.shape[1:], BF), vm(w_down.shape[1:], BF),
        vm((2, 4, 4 * rows, half + 128), BF),
        vm((rows, 128), F32), vm((rows, 128), F32),
        vm((4 * rows, wide), BF),
        vm((4, 4 * rows, half), F32),
        vm((4, 4 * rows, half), BF), vm((4, 4 * rows, half), BF),
        vm((4, 2 * rows, quarter), BF), vm((4, 2 * rows, quarter), BF),
        vm((4, 2 * rows, quarter), BF), vm((4, 2 * rows, quarter), BF),
        vm((4, rows, quarter), BF), vm((4, rows, quarter), BF),
        vm((4, rows, quarter), BF), vm((4, rows, quarter), BF),
        vm((4, rows, half), BF), vm((4, rows, half), BF),
        vm((16, PIECE, out_cache.shape[1]), BF), vm((16, PIECE, out_cache.shape[1] - 128), BF),
        pltpu.SemaphoreType.DMA((3,)),
        pltpu.SemaphoreType.DMA((13, 4)), pltpu.SemaphoreType.DMA((13, 4)),
        pltpu.SemaphoreType.DMA((16,)), pltpu.SemaphoreType.DMA((16,)),
        pltpu.SemaphoreType.DMA((16,)), pltpu.SemaphoreType.DMA((16,)),
        pltpu.SemaphoreType.DMA,
    ]
    inside = pl.BlockSpec(memory_space=pltpu.VMEM)
    outside = pl.BlockSpec(memory_space=pl.ANY)
    return pl.pallas_call(
        exchange_kernel,
        out_shape=(
            jax.ShapeDtypeStruct((steps, req, half), BF),
            jax.ShapeDtypeStruct((out_cache.shape[0], out_cache.shape[1] - 128), BF),
        ),
        in_specs=[inside] * 5 + [outside] * 3,
        out_specs=(inside, inside),
        scratch_shapes=scratch,
        compiler_params=pltpu.CompilerParams(
            collective_id=0, has_side_effects=True, vmem_limit_bytes=56 * 1024 * 1024
        ),
    )(hidden, gain, routes, logits, out_cache, w_gate, w_up, w_down)


def body_slots(
    queries, new_kv, kv_pool, block_table, lengths, new_group, hidden_rows, norm_gain,
    routes, route_logits, w_gate, w_up, w_down,
):
    steps, req, _, kv_width = new_kv.shape
    blocks, block_tokens = kv_pool.shape[:2]
    span = block_table.shape[1] * block_tokens
    kv_local = kv_width // HD
    position = lengths[None, :] + jnp.arange(steps)[:, None]
    target = (
        block_table[jnp.arange(req)[None, :], position // block_tokens] * block_tokens
        + position % block_tokens
    )
    pool_now = (
        kv_pool.reshape(blocks * block_tokens, 2, kv_width)
        .at[target.reshape(-1)]
        .set(new_kv.reshape(steps * req, 2, kv_width))
        .reshape(kv_pool.shape)
    )
    slot = jnp.argmax((new_group != lax.axis_index("dec")).astype(jnp.int32))
    depart = block_table[slot]
    outgoing = pool_now[depart].reshape(span, 2 * kv_width)
    head = jnp.broadcast_to(new_group[slot].astype(BF), (span, 128))
    moe_out, incoming = exchange(
        hidden_rows, norm_gain.astype(F32).reshape(2, -1), routes, route_logits,
        jnp.concatenate([outgoing, head], axis=1), w_gate, w_up, w_down,
    )
    cached = pool_now[block_table].reshape(req, span, 2, kv_local, HD)
    keys, values = cached[:, :, 0], cached[:, :, 1]
    grouped = queries.reshape(steps, req, kv_local, -1, HD)
    scores = jnp.einsum("trkgd,rlkd->rktgl", grouped, keys, preferred_element_type=F32)
    scores = scores * (1.0 / math.sqrt(HD))
    visible = jnp.arange(span)[None, None, :] < (position.T + 1)[:, :, None]
    visible = visible[:, None, :, None, :]
    masked = jnp.where(visible, scores, -1e30)
    weights = jnp.where(visible, jnp.exp(masked - jnp.max(masked, axis=-1, keepdims=True)), 0.0)
    shares = (weights / jnp.sum(weights, axis=-1, keepdims=True)).astype(BF)
    mixed = jnp.einsum("rktgl,rlkd->trkgd", shares, values, preferred_element_type=F32)
    attn_out = mixed.astype(BF).reshape(steps, req, -1)
    pool_after = pool_now.at[depart].set(incoming.reshape(-1, block_tokens, 2, kv_width))
    return attn_out, moe_out, pool_after


def solution(mesh):
    sized = mesh.shape["dec"] == 16 and mesh.shape["tp"] == 2
    body = body_slots if sized else body_general
    return jax.shard_map(
        body,
        mesh=mesh,
        in_specs=(
            P(None, "dec", "tp"),
            P(None, "dec", None, "tp"),
            P("dec", None, None, "tp"),
            P("dec", None),
            P("dec"),
            P("dec"),
            P(None, "dec", "tp"),
            P(),
            P(None, "dec", None),
            P(None, "dec", None),
            P("dec", None, "tp"),
            P("dec", None, "tp"),
            P("dec", "tp", None),
        ),
        out_specs=(P(None, "dec", "tp"), P(None, "dec", "tp"), P("dec", None, None, "tp")),
        check_vma=False,
    )
```

profile of v0, /device:TPU:0, one launch (start us, length us, event | category | flops | bytes accessed | tf_op | source)
XLA Modules:
  0.0 139.0 jit_solution(11494460638824997369)
XLA Ops:
  0.6 0.0 copy-start
  0.6 0.0 copy-start.1
  0.7 0.0 copy-start.6
  0.7 6.1 %copy.60 = bf16[64,32,2,256]{3,2,1,0:T(2,128)(2,1)} copy(bf16[64,32,2,256]{3,2,1,0:T(2,128)(2,1)} %param.15) | data formatting | bytes 4194304
  6.7 0.0 copy-start.4
  6.7 0.0 copy-done.6
  6.8 0.1 add.149
  6.9 0.1 reshape.265
  6.9 0.0 copy-done.1
  6.9 0.7 gather_fusion
  7.6 0.0 copy-done.4
  7.6 4.2 %scatter_fusion = bf16[2048,2,256]{2,1,0:T(2,128)(2,1)} fusion(bf16[2048,2,256]{2,1,0:T(2,128)(2,1)} %bitcast, s32[32]{0:T(128)S(1)} %fusion.18, bf16[32,2,256]{2,1,0:T(2,128)(2,1)S(1)} %bitcast.54), kind=kCustom, calls=%fused_computation.3 | custom fusion | bytes 98432 | tf_op jit(solution)/shard_map/scatter | solution.py:461
  11.8 1.9 %copy.31 = bf16[2048,2,256]{2,0,1:T(8,128)(2,1)S(1)} copy(bf16[2048,2,256]{2,1,0:T(2,128)(2,1)} %scatter_fusion) | data formatting | bytes 4194304 | tf_op jit(solution)/shard_map/scatter | solution.py:461
  13.7 0.1 reshape.273
  13.8 2.0 %gather_fusion.1 = bf16[64,32,2,256]{3,1,2,0:T(8,128)(2,1)} fusion(bf16[64,32,2,256]{3,1,0,2:T(8,128)(2,1)S(1)} %bitcast.49, s32[1024]{0:T(1024)S(1)} %pad_clamp_fusion.1), kind=kCustom, calls=%fused_computation.1 | custom fusion | bytes 4194560 | tf_op jit(solution)/shard_map/gather | solution.py:472
  15.8 3.1 %copy.32 = bf16[64,32,2,256]{3,1,0,2:T(8,128)(2,1)} copy(bf16[64,32,2,256]{3,1,2,0:T(8,128)(2,1)} %gather_fusion.1) | data formatting | bytes 4194304 | tf_op jit(solution)/shard_map/gather | solution.py:472
  18.9 4.0 %reshape.256 = bf16[8,256,2,2,128]{4,3,1,0,2:T(2,128)(2,1)} reshape(bf16[64,32,2,256]{3,1,0,2:T(8,128)(2,1)} %copy.32) | data formatting | bytes 4194304 | tf_op jit(solution)/shard_map/reshape | solution.py:472
  22.9 3.5 %fusion.20 = (bf16[8,256,1,2,128]{4,3,1,0,2:T(2,128)(2,1)}, bf16[8,256,1,2,128]{4,3,1,0,2:T(2,128)(2,1)S(1)}) fusion(bf16[8,256,2,2,128]{4,3,1,0,2:T(2,128)(2,1)} %reshape.256), kind=kLoop, calls=%fused_computation.49 | loop fusion | bytes 4194304 | tf_op jit(solution)/shard_map/slice | solution.py:473
  26.3 0.1 add_add_fusion
  26.4 0.1 iota_compare_fusion
  26.5 0.0 copy-done
  26.5 2.8 %fusion.21 = (f32[8,2,4,16]{3,2,1,0:T(4,128)S(1)}, f32[8,2,4,16,256]{4,3,2,1,0:T(8,128)}) fusion(pred[8,4,256]{2,1,0:T(4,128)(4,1)S(1)} %iota_compare_fusion, bf16[8,256,1,2,128]{4,3,1,0,2:T(2,128)(2,1)} %get-tuple-element.18, bf16[4,8,2,16,128]{4,1,3,2,0:T(8,128)(2,1)S(1)} %bitcast.48), kind=kOutput, calls=%fused_computation.50 | convolution fusion | flops 68419840 | bytes 2371584 | tf_op jit(solution)/shard_map/sub | solution.py:480
  29.3 0.0 copy-start.5
  29.3 0.0 copy-start.7
  29.3 1.6 %fusion.6 = bf16[4,8,2,16,128]{4,3,0,2,1:T(8,128)(2,1)S(1)} fusion(bf16[8,256,1,2,128]{4,3,1,0,2:T(2,128)(2,1)S(1)} %get-tuple-element.19, f32[8,2,4,16,256]{4,3,2,1,0:T(8,128)} %get-tuple-element.21, f32[8,2,4,16]{3,2,1,0:T(4,128)S(1)} %get-tuple-element.20), kind=kOutput, calls=%fused_computation.13 | convolution fusion | flops 67764224 | bytes 2363392 | tf_op jit(solution)/shard_map/rktgl,rlkd->trkgd/dot_general | solution.py:482
  31.0 0.8 reshape.258
  31.8 0.0 copy-done.5
  31.8 0.6 reshape.264.gain
  32.4 0.0 copy-done.7
  32.4 0.7 fusion.16
  35.3 0.6 gather_fusion.2
  35.8 0.3 copy.37
  36.2 0.6 dynamic_slice.7
  37.4 0.8 concatenate.7.out_cache
  38.2 91.2 %shard_map.148 = (bf16[4,8,2048]{2,1,0:T(8,128)(2,1)}, bf16[256,512]{1,0:T(8,128)(2,1)}) custom-call(bf16[4,8,2048]{2,1,0:T(8,128)(2,1)} %hid.1, f32[2,2048]{1,0:T(2,128)} %reshape.264.gain, s32[4,8,8]{2,1,0:T(8,128)} %routes.1, f32[4,8,8]{2,1,0:T(8,128)} %logits.1, bf16[256,640]{1,0:T(8,128)(2,1)} %concatenate.7.out_cache, bf16[1,4096,768]{2,1,0:T(8,128)(2,1)} %wg_hbm.1, ...), custom_call_target="tpu_custom_call" | custom-call | tf_op jit(solution)/shard_map/pallas_call | solution.py:430
  129.3 0.0 copy-start.2
  129.3 1.6 %copy.38 = bf16[64,32,2,256]{3,1,2,0:T(8,128)(2,1)} copy(bf16[64,32,2,256]{3,1,0,2:T(8,128)(2,1)S(1)} %bitcast.51) | data formatting | bytes 4194304 | tf_op jit(solution)/shard_map/reshape | solution.py:462
  130.9 0.0 copy-done.2
  130.9 0.1 reshape.299
  131.0 2.2 %scatter_fusion.1 = bf16[64,32,2,256]{3,1,2,0:T(8,128)(2,1)} fusion(bf16[64,32,2,256]{3,1,2,0:T(8,128)(2,1)} %copy.38, s32[8]{0:T(128)S(1)} %fusion.19, bf16[8,32,2,256]{3,1,2,0:T(8,128)(2,1)S(1)} %copy.39), kind=kCustom, calls=%fused_computation.4 | custom fusion | bytes 786464 | tf_op jit(solution)/shard_map/scatter | solution.py:484
  133.2 0.0 copy-start.3
  133.2 5.1 %copy.40 = bf16[64,32,2,256]{3,2,1,0:T(2,128)(2,1)} copy(bf16[64,32,2,256]{3,1,2,0:T(8,128)(2,1)} %scatter_fusion.1) | data formatting | bytes 4194304
  138.3 0.0 copy-done.3
  138.3 0.7 copy.61
  (10 shorter events, 0.1 us)
Async XLA Ops:
  0.6 25.9 %copy-start = (bf16[4,8,4096]{2,1,0:T(8,128)(2,1)S(1)}, bf16[4,8,4096]{2,1,0:T(8,128)(2,1)}, u32[]{:S(2)}) copy-start(bf16[4,8,4096]{2,1,0:T(8,128)(2,1)} %param.13) | copy-start | bytes 786436
  0.6 6.3 %copy-start.1 = (s32[8,8]{1,0:T(8,128)S(1)}, s32[8,8]{1,0:T(8,128)}, u32[]{:S(2)}) copy-start(s32[8,8]{1,0:T(8,128)} %param.16) | copy-start | bytes 772
  0.7 6.1 %copy-start.6 = (s32[8]{0:T(128)S(1)}, s32[8]{0:T(128)}, u32[]{:S(2)}) copy-start(s32[8]{0:T(128)} %param.17) | copy-start | bytes 100
  6.7 0.9 copy-start.4
  29.3 2.5 %copy-start.5 = (bf16[4096]{0:T(1024)(128)(2,1)S(1)}, bf16[4096]{0:T(1024)(128)(2,1)}, u32[]{:S(2)}) copy-start(bf16[4096]{0:T(1024)(128)(2,1)} %param.20) | copy-start | bytes 24580
  29.3 3.1 %copy-start.7 = (s32[8]{0:T(128)S(1)}, s32[8]{0:T(128)}, u32[]{:S(2)}) copy-start(s32[8]{0:T(128)} %param.18) | copy-start | bytes 100
  129.3 1.6 %copy-start.2 = (bf16[256,512]{1,0:T(8,128)(2,1)S(1)}, bf16[256,512]{1,0:T(8,128)(2,1)}, u32[]{:S(2)}) copy-start(bf16[256,512]{1,0:T(8,128)(2,1)} %get-tuple-element.8) | copy-start | bytes 786436
  133.2 5.1 %copy-start.3 = (bf16[4,8,2048]{2,1,0:T(8,128)(2,1)S(1)}, bf16[4,8,2048]{2,1,0:T(8,128)(2,1)}, u32[]{:S(2)}) copy-start(bf16[4,8,2048]{2,1,0:T(8,128)(2,1)} %get-tuple-element.26) | copy-start | bytes 393220
where the time goes:
time: 140 us; the launch traced here: 139 us
  Pallas kernels  91.2 us (65%)
  local copies, waits for them, and re-layouts  38.9 us (28%)
  matrix products  4.43 us (3%)
  between operations  3.53 us (3%)
    pallas_call x1, Pallas kernels, exchange(): pl.pallas_call(exchange_kernel, out_shape=(jax.ShapeDtypeStruct((steps, r...  91.2 us
    unnamed x20, local copies, waits for them, and re-layouts  11.9 us
    scatter x2, local copies, waits for them, and re-layouts, body_slots(): pool_now = kv_pool.reshape(blocks * block_tokens, 2, kv_width).at[target....  6.02 us
    gather x2, local copies, waits for them, and re-layouts, body_slots(): cached = pool_now[block_table].reshape(req, span, 2, kv_local, HD)  5.15 us
    reshape x1, local copies, waits for them, and re-layouts, body_slots(): cached = pool_now[block_table].reshape(req, span, 2, kv_local, HD)  3.95 us
    slice x1, local copies, waits for them, and re-layouts, body_slots(): keys, values = (cached[:, :, 0], cached[:, :, 1])  3.47 us
    sub x1, matrix products, body_slots(): masked - jnp.max(masked, axis=-1, keepdims=True)  2.82 us

commit v1 on v0

--- a/solution.py
+++ b/solution.py
@@ -156,7 +156,8 @@
 F32 = jnp.float32
 BF = jnp.bfloat16
 SS, ZG, X1, Y1, X2, Y2, SIB, TP, RA, RB, RA2, RB2, RZ = range(13)
-PIECE = 16
+PIECE = 64
+HEAD = 16
 
 
 def exchange_kernel(
@@ -246,12 +247,12 @@
     for m in range(1, count):
         peer = (me + m) % count
         copy = pltpu.make_async_remote_copy(
-            src_ref=out_cache.at[pl.ds(peer * PIECE, PIECE)], dst_ref=mig_in.at[m],
+            src_ref=out_cache.at[peer], dst_ref=mig_in.at[m],
             send_sem=m_s1.at[m], recv_sem=m_r1.at[m], device_id={"dec": peer}, device_id_type=MESH,
         )
         copy.start()
         first.append(copy)
-    mig_in[0] = out_cache[pl.ds(me * PIECE, PIECE)]
+    mig_in[0] = out_cache[me]
 
     def gather(q):
         if q < 3:
@@ -351,8 +352,8 @@
         wanted = peer.astype(F32)
         chosen = jnp.zeros((PIECE, width), F32)
         for n in range(count):
-            head = mig_in[n, :, width : width + 1].astype(F32)
-            chosen = jnp.where(head == wanted, mig_in[n, :, 0:width].astype(F32), chosen)
+            head = mig_in[n, PIECE:, :].astype(F32)[0:1]
+            chosen = jnp.where(head == wanted, mig_in[n, 0:PIECE].astype(F32), chosen)
         mig_out[m] = chosen.astype(BF)
         where = inc_ref.at[pl.ds(me * PIECE, PIECE)]
         if m:
@@ -418,7 +419,7 @@
         vm((4, rows, quarter), BF), vm((4, rows, quarter), BF),
         vm((4, rows, quarter), BF), vm((4, rows, quarter), BF),
         vm((4, rows, half), BF), vm((4, rows, half), BF),
-        vm((16, PIECE, out_cache.shape[1]), BF), vm((16, PIECE, out_cache.shape[1] - 128), BF),
+        vm(out_cache.shape, BF), vm((16, PIECE, 128), BF),
         pltpu.SemaphoreType.DMA((3,)),
         pltpu.SemaphoreType.DMA((13, 4)), pltpu.SemaphoreType.DMA((13, 4)),
         pltpu.SemaphoreType.DMA((16,)), pltpu.SemaphoreType.DMA((16,)),
@@ -431,7 +432,7 @@
         exchange_kernel,
         out_shape=(
             jax.ShapeDtypeStruct((steps, req, half), BF),
-            jax.ShapeDtypeStruct((out_cache.shape[0], out_cache.shape[1] - 128), BF),
+            jax.ShapeDtypeStruct((16 * PIECE, 128), BF),
         ),
         in_specs=[inside] * 5 + [outside] * 3,
         out_specs=(inside, inside),
@@ -442,46 +443,147 @@
     )(hidden, gain, routes, logits, out_cache, w_gate, w_up, w_down)
 
 
+def leaving_slot(moves):
+    me = lax.axis_index("dec")
+    slot = jnp.int32(0)
+    for r in range(1, moves.shape[0]):
+        slot = jnp.where(moves[r] != me, r, slot)
+    return slot
+
+
+def cache_kernel(
+    table, lengths, moves, q_ref, new_ref, pool, attn_ref, pool_out, outgoing,
+    cache, q_wide, o_wide, read_sem, write_sem,
+):
+    req, blocks = table.shape
+    rows = cache.shape[1] // blocks
+    reads = [[None] * blocks for _ in range(req)]
+    for r in range(req):
+        for j in range(blocks):
+            at = pl.ds(pl.multiple_of(table[r, j] * rows, rows), rows)
+            reads[r][j] = pltpu.make_async_copy(
+                pool.at[at], cache.at[r, pl.ds(j * rows, rows)], read_sem.at[r, j]
+            )
+            reads[r][j].start()
+    q_wide[...] = q_ref[...].reshape(q_wide.shape).astype(F32)
+    heads = q_ref.shape[1]
+    steps = q_ref.shape[0]
+    kv_local = 2
+    shape = (steps * heads, cache.shape[1])
+    row = lax.broadcasted_iota(jnp.int32, shape, 0)
+    col = lax.broadcasted_iota(jnp.int32, shape, 1)
+    matching = (col % 4) == 2 * ((row % heads) // (heads // kv_local))
+    offset = jnp.where(matching, col // 4 - row // heads, 1 << 20)
+    part = lax.broadcasted_iota(jnp.int32, (16, 128), 0) // 4
+    writes = []
+    for r in range(req):
+        for j in range(blocks):
+            reads[r][j].wait()
+        for t in range(steps):
+            place = lengths[r] + t
+            window = pl.ds(pl.multiple_of((place // 4) * 16, 16), 16)
+            old = cache[r, window].astype(F32)
+            cache[r, window] = jnp.where(part == place % 4, new_ref[t, r], old).astype(BF)
+        for j in range(blocks):
+            at = pl.ds(pl.multiple_of(table[r, j] * rows, rows), rows)
+            copy = pltpu.make_async_copy(
+                cache.at[r, pl.ds(j * rows, rows)], pool_out.at[at], write_sem.at[r, j]
+            )
+            copy.start()
+            writes.append(copy)
+    slot = leaving_slot(moves)
+    target = moves[slot].astype(F32)
+    for n in range(outgoing.shape[0]):
+        outgoing[n, 0:PIECE] = cache[slot, pl.ds(n * PIECE, PIECE)]
+        outgoing[n, PIECE:] = jnp.full((HEAD, 128), target, F32).astype(BF)
+    for r in range(req):
+        kv = cache[r]
+        query = q_wide[pl.ds(r, steps * heads, stride=req), :].astype(BF)
+        scores = lax.dot_general(
+            query, kv, (((1,), (1,)), ((), ())), preferred_element_type=F32
+        ) * (1.0 / math.sqrt(HD))
+        visible = offset < lengths[r] + 1
+        masked = jnp.where(visible, scores, -1e30)
+        grown = jnp.where(visible, jnp.exp(masked - jnp.max(masked, axis=-1, keepdims=True)), 0.0)
+        shares = grown / jnp.sum(grown, axis=-1, keepdims=True)
+        shares = pltpu.roll(shares, 1, 1).astype(BF)
+        o_wide[pl.ds(r, steps * heads, stride=req), :] = jnp.dot(
+            shares, kv, preferred_element_type=F32
+        )
+    attn_ref[...] = o_wide[...].astype(BF).reshape(attn_ref.shape)
+    for copy in writes:
+        copy.wait()
+
+
+def place_kernel(table, moves, incoming, pool, pool_out, sem):
+    del pool
+    slot = leaving_slot(moves)
+    blocks = table.shape[1]
+    rows = incoming.shape[0] // blocks
+    copies = []
+    for j in range(blocks):
+        at = pl.ds(pl.multiple_of(table[slot, j] * rows, rows), rows)
+        copy = pltpu.make_async_copy(incoming.at[pl.ds(j * rows, rows)], pool_out.at[at], sem.at[j])
+        copy.start()
+        copies.append(copy)
+    for copy in copies:
+        copy.wait()
+
+
+def dense_rows(values):
+    lead = values.shape[:-2]
+    n = len(lead)
+    split = values.reshape(*lead, 2, values.shape[-1] // HD, HD)
+    return split.transpose(*range(n), n + 1, n, n + 2)
+
+
 def body_slots(
     queries, new_kv, kv_pool, block_table, lengths, new_group, hidden_rows, norm_gain,
     routes, route_logits, w_gate, w_up, w_down,
 ):
     steps, req, _, kv_width = new_kv.shape
     blocks, block_tokens = kv_pool.shape[:2]
-    span = block_table.shape[1] * block_tokens
-    kv_local = kv_width // HD
-    position = lengths[None, :] + jnp.arange(steps)[:, None]
-    target = (
-        block_table[jnp.arange(req)[None, :], position // block_tokens] * block_tokens
-        + position % block_tokens
-    )
-    pool_now = (
-        kv_pool.reshape(blocks * block_tokens, 2, kv_width)
-        .at[target.reshape(-1)]
-        .set(new_kv.reshape(steps * req, 2, kv_width))
-        .reshape(kv_pool.shape)
-    )
-    slot = jnp.argmax((new_group != lax.axis_index("dec")).astype(jnp.int32))
-    depart = block_table[slot]
-    outgoing = pool_now[depart].reshape(span, 2 * kv_width)
-    head = jnp.broadcast_to(new_group[slot].astype(BF), (span, 128))
+    span_rows = block_table.shape[1] * block_tokens * 4
+    heads = queries.shape[2] // HD
+    pool = dense_rows(kv_pool).reshape(-1, HD)
+    new = jnp.tile(dense_rows(new_kv).reshape(steps, req, 4, HD), (1, 1, 4, 1)).astype(F32)
+    q = queries.reshape(steps, req, heads, HD).transpose(0, 2, 1, 3)
+    scalar = pl.BlockSpec(memory_space=pltpu.SMEM)
+    inside = pl.BlockSpec(memory_space=pltpu.VMEM)
+    outside = pl.BlockSpec(memory_space=pl.ANY)
+    attn, pool_now, outgoing = pl.pallas_call(
+        cache_kernel,
+        out_shape=(
+            jax.ShapeDtypeStruct(q.shape, BF),
+            jax.ShapeDtypeStruct(pool.shape, BF),
+            jax.ShapeDtypeStruct((16, PIECE + HEAD, HD), BF),
+        ),
+        in_specs=[scalar] * 3 + [inside] * 2 + [outside],
+        out_specs=(inside, outside, inside),
+        scratch_shapes=[
+            pltpu.VMEM((req, span_rows, HD), BF),
+            pltpu.VMEM((steps * heads * req, HD), F32),
+            pltpu.VMEM((steps * heads * req, HD), F32),
+            pltpu.SemaphoreType.DMA(block_table.shape),
+            pltpu.SemaphoreType.DMA(block_table.shape),
+        ],
+        compiler_params=pltpu.CompilerParams(vmem_limit_bytes=32 * 1024 * 1024),
+    )(block_table, lengths, new_group, q, new, pool)
     moe_out, incoming = exchange(
         hidden_rows, norm_gain.astype(F32).reshape(2, -1), routes, route_logits,
-        jnp.concatenate([outgoing, head], axis=1), w_gate, w_up, w_down,
+        outgoing, w_gate, w_up, w_down,
     )
-    cached = pool_now[block_table].reshape(req, span, 2, kv_local, HD)
-    keys, values = cached[:, :, 0], cached[:, :, 1]
-    grouped = queries.reshape(steps, req, kv_local, -1, HD)
-    scores = jnp.einsum("trkgd,rlkd->rktgl", grouped, keys, preferred_element_type=F32)
-    scores = scores * (1.0 / math.sqrt(HD))
-    visible = jnp.arange(span)[None, None, :] < (position.T + 1)[:, :, None]
-    visible = visible[:, None, :, None, :]
-    masked = jnp.where(visible, scores, -1e30)
-    weights = jnp.where(visible, jnp.exp(masked - jnp.max(masked, axis=-1, keepdims=True)), 0.0)
-    shares = (weights / jnp.sum(weights, axis=-1, keepdims=True)).astype(BF)
-    mixed = jnp.einsum("rktgl,rlkd->trkgd", shares, values, preferred_element_type=F32)
-    attn_out = mixed.astype(BF).reshape(steps, req, -1)
-    pool_after = pool_now.at[depart].set(incoming.reshape(-1, block_tokens, 2, kv_width))
+    pool_after = pl.pallas_call(
+        place_kernel,
+        out_shape=jax.ShapeDtypeStruct(pool.shape, BF),
+        in_specs=[scalar] * 2 + [outside] * 2,
+        out_specs=outside,
+        scratch_shapes=[pltpu.SemaphoreType.DMA((block_table.shape[1],))],
+        input_output_aliases={3: 0},
+    )(block_table, new_group, incoming, pool_now)
+    back = pool_after.reshape(blocks, block_tokens, kv_width // HD, 2, HD)
+    pool_after = back.transpose(0, 1, 3, 2, 4).reshape(kv_pool.shape)
+    attn_out = attn.transpose(0, 2, 1, 3).reshape(queries.shape)
     return attn_out, moe_out, pool_after
 
 

time: 140 us -> 120 us (0.86)
  local copies, waits for them, and re-layouts: 38.9 us -> 8.99 us
  Pallas kernels: 91.2 us -> 109 us
  matrix products: 4.43 us -> 0 us
  between operations: 3.53 us -> 0.7 us
    pallas_call x0 -> x2, Pallas kernels: none -> 20.8 us  [the longest x1 10.9 us: body_slots(): pl.pallas_call(cache_kernel, out_shape=(jax.ShapeDtypeStruct(q.shape, BF)...]
    scatter x3 -> x0, local copies, waits for them, and re-layouts: 8.2 us -> none  [the longest x2 6.02 us: body_slots(): pool_now = kv_pool.reshape(blocks * block_tokens, 2, kv_width).at[target....]
    gather x5 -> x0, local copies, waits for them, and re-layouts: 6.66 us -> none  [the longest x2 5.15 us: body_slots(): cached = pool_now[block_table].reshape(req, span, 2, kv_local, HD)]
    reshape x5 -> x0, local copies, waits for them, and re-layouts: 6.43 us -> none  [the longest x1 3.95 us: body_slots(): cached = pool_now[block_table].reshape(req, span, 2, kv_local, HD)]
    unnamed x20 -> x13, local copies, waits for them, and re-layouts: 11.9 us -> 6.82 us
    slice x1 -> x0, local copies, waits for them, and re-layouts: 3.47 us -> none  [body_slots(): keys, values = (cached[:, :, 0], cached[:, :, 1])]
    sub x1 -> x0, matrix products: 2.82 us -> none  [body_slots(): masked - jnp.max(masked, axis=-1, keepdims=True)]
    pallas_call x1, Pallas kernels: 91.2 us -> 88.5 us  [exchange(): pl.pallas_call(exchange_kernel, out_shape=(jax.ShapeDtypeStruct((steps, r...]
where the time goes in v1:
time: 120 us; the launch traced here: 119 us
  Pallas kernels  109 us (91%)
  local copies, waits for them, and re-layouts  8.99 us (7%)
    pallas_call x1, Pallas kernels, exchange(): pl.pallas_call(exchange_kernel, out_shape=(jax.ShapeDtypeStruct((steps, r...  88.5 us
    pallas_call x1, Pallas kernels, body_slots(): pl.pallas_call(cache_kernel, out_shape=(jax.ShapeDtypeStruct(q.shape, BF)...  10.9 us
    pallas_call x1, Pallas kernels, body_slots(): pl.pallas_call(place_kernel, out_shape=jax.ShapeDtypeStruct(pool.shape, B...  9.87 us
    unnamed x13, local copies, waits for them, and re-layouts  6.82 us

profile of v1, /device:TPU:0, one launch (start us, length us, event | category | flops | bytes accessed | tf_op | source)
XLA Modules:
  0.0 119.0 jit_solution(3352748589924443197)
XLA Ops:
  0.6 1.3 %reshape.49.gain = f32[2,2048]{1,0:T(2,128)} reshape(bf16[4096]{0:T(1024)(128)(2,1)} %param.20) | data formatting | bytes 24576 | tf_op jit(solution)/shard_map/reshape | solution.py:573
  1.9 0.8 reshape.51
  2.8 0.0 copy-start
  2.8 1.6 %copy-done = bf16[64,32,2,256]{3,2,1,0:T(2,128)(2,1)S(1)} copy-done((bf16[64,32,2,256]{3,2,1,0:T(2,128)(2,1)S(1)}, bf16[64,32,2,256]{3,2,1,0:T(2,128)(2,1)}, u32[]{:S(2)}) %copy-start) | copy-done | bytes 2097176
  4.4 0.0 copy-start.2
  4.4 0.9 copy-done.2
  5.4 0.0 copy-start.3
  5.4 0.7 copy-done.3
  6.1 0.0 copy-start.4
  6.1 0.7 copy-done.4
  6.7 0.0 copy-start.5
  6.7 0.7 copy-done.5
  7.4 10.9 %shard_map.148 = (bf16[4,32,8,128]{3,2,1,0:T(8,128)(2,1)}, bf16[8192,128]{1,0:T(8,128)(2,1)}, bf16[16,80,128]{2,1,0:T(8,128)(2,1)S(1)}) custom-call(s32[8,8]{1,0:T(8,128)S(1)} %copy-done.3, s32[8]{0:T(128)S(1)} %copy-done.5, s32[8]{0:T(128)S(1)} %copy-done.4, bf16[4,32,8,128]{3,2,1,0:T(8,128)(2,1)S(1)} %bitcast.22, f32[4,8,16,128]{3,2,1,0:T(8,128)S(1)} %bitcast.21, ...), custom_call_target="tpu_custom_call" | custom-call | tf_op jit(solution)/shard_map/pallas_call | solution.py:554
  18.3 0.0 copy-start.1
  18.3 0.7 copy-done.1
  19.1 88.5 %shard_map.149 = (bf16[4,8,2048]{2,1,0:T(8,128)(2,1)}, bf16[1024,128]{1,0:T(8,128)(2,1)}) custom-call(bf16[4,8,2048]{2,1,0:T(8,128)(2,1)} %hid.1, f32[2,2048]{1,0:T(2,128)} %reshape.49.gain, s32[4,8,8]{2,1,0:T(8,128)} %routes.1, f32[4,8,8]{2,1,0:T(8,128)} %logits.1, bf16[16,80,128]{2,1,0:T(8,128)(2,1)} %copy-done.1, bf16[1,4096,768]{2,1,0:T(8,128)(2,1)} %wg_hbm.1, ...), custom_call_target="tpu_custom_call" | custom-call | tf_op jit(solution)/shard_map/pallas_call | solution.py:431
  107.5 9.9 %shard_map.150 = bf16[8192,128]{1,0:T(8,128)(2,1)} custom-call(s32[8,8]{1,0:T(8,128)} %table.3, s32[8]{0:T(128)} %moves.3, bf16[1024,128]{1,0:T(8,128)(2,1)} %get-tuple-element.11.incoming, bf16[8192,128]{1,0:T(8,128)(2,1)} %get-tuple-element.12.pool), custom_call_target="tpu_custom_call", output_to_operand_aliasing={{}: (3, {})} | custom-call | tf_op jit(solution)/shard_map/pallas_call | solution.py:576
  117.4 1.6 %copy.31 = bf16[4,8,2048]{2,1,0:T(8,128)(2,1)} copy(bf16[4,8,2048]{2,1,0:T(8,128)(2,1)} %get-tuple-element.17) | data formatting | bytes 262144
  (3 shorter events, 0.1 us)
Async XLA Ops:
  2.8 1.6 %copy-start = (bf16[64,32,2,256]{3,2,1,0:T(2,128)(2,1)S(1)}, bf16[64,32,2,256]{3,2,1,0:T(2,128)(2,1)}, u32[]{:S(2)}) copy-start(bf16[64,32,2,256]{3,2,1,0:T(2,128)(2,1)} %param.15) | copy-start | bytes 6291460
  4.4 0.9 copy-start.2
  5.4 0.7 copy-start.3
  6.1 0.7 copy-start.4
  6.7 0.7 copy-start.5
  18.3 0.7 copy-start.1

commit v2 on v1

--- a/solution.py
+++ b/solution.py
@@ -156,6 +156,7 @@
 F32 = jnp.float32
 BF = jnp.bfloat16
 SS, ZG, X1, Y1, X2, Y2, SIB, TP, RA, RB, RA2, RB2, RZ = range(13)
+SIBS = (SIB, 13, 14, 15)
 PIECE = 64
 HEAD = 16
 
@@ -243,6 +244,108 @@
     spread(0)
     zg = {q: go(remote(ZG, q, slot(0, 0), slot(q, 0), {"dec": z_peers[q]})) for q in (1, 2, 3)}
 
+    def relay(q, n):
+        part = slot(q, n)
+        return go(remote(SIBS[n], q, part, part, {"tp": 1 - core}))
+
+    relays, crossed = {}, {}
+
+    def gather_a(q):
+        relays[q] = [relay(q, 0)]
+        y1[q].wait_recv()
+        x2 = go(remote(X2, q, slot(q, 2, 0, quarter), slot(q, 3, 0, quarter), {"dec": x_peer}))
+        x1[q].wait_recv()
+        y2 = go(remote(Y2, q, slot(q, 1, quarter), slot(q, 3, quarter), {"dec": y_peer}))
+        crossed[q] = (x2, y2)
+        relays[q] += [relay(q, 1), relay(q, 2)]
+        if q < 3:
+            zg[q + 1].wait_recv()
+            spread(q + 1)
+
+    def gather_b(q):
+        for copy in crossed[q]:
+            copy.wait_recv()
+        relays[q].append(relay(q, 3))
+        for copy in relays[q]:
+            copy.wait_recv()
+
+    def apply(q):
+        if q == 0:
+            weights[0].wait()
+            weights[1].wait()
+
+        @pl.loop(0, act.shape[1] // 256)
+        def _(i):
+            cols = pl.ds(pl.multiple_of(i * 256, 256), 256)
+
+            def product(w):
+                return jnp.dot(
+                    gath[0, q, :, 0:half], w[0:half, cols], preferred_element_type=F32
+                ) + jnp.dot(
+                    gath[1, q, :, 0:half], w[half : 2 * half, cols], preferred_element_type=F32
+                )
+
+            g = product(wg)
+            act[:, cols] = (g / (1.0 + jnp.exp(-g)) * product(wu)).astype(BF)
+
+        if q == 0:
+            weights[2].wait()
+        probs = gath[0, q, :, half:].astype(F32)
+        lanes = lax.broadcasted_iota(jnp.int32, probs.shape, 1)
+        mine = (lanes == me) | (lanes == me + 16)
+        weight = jnp.sum(jnp.where(mine, probs, 0.0), axis=-1, keepdims=True)
+        step = 512
+
+        @pl.loop(0, half // step)
+        def _(i):
+            to = pl.ds(pl.multiple_of(i * step, step), step)
+            cols = pl.ds(pl.multiple_of((1 - core) * half + i * step, step), step)
+            tp_out[q, :, to] = (
+                jnp.dot(act[...], wd[:, cols], preferred_element_type=F32) * weight
+            ).astype(BF)
+
+        copy = go(remote(TP, q, tp_out.at[q], tp_in.at[q], {"tp": 1 - core}))
+
+        @pl.loop(0, half // step)
+        def _(i):
+            to = pl.ds(pl.multiple_of(i * step, step), step)
+            cols = pl.ds(pl.multiple_of(core * half + i * step, step), step)
+            acc[q, :, to] = jnp.dot(act[...], wd[:, cols], preferred_element_type=F32) * weight
+
+        return copy
+
+    ra, rb, ra2, rb2, rz = {}, {}, {}, {}, {}
+    r = rows
+
+    def fold1(q, copy):
+        copy.wait_recv()
+        acc[q] = acc[q] + tp_in[q].astype(F32)
+        a_out[q, 0:r] = acc[q, r : 2 * r, 0:quarter].astype(BF)
+        a_out[q, r : 2 * r] = acc[q, 3 * r : 4 * r, 0:quarter].astype(BF)
+        ra[q] = go(remote(RA, q, a_out.at[q], a_in.at[q], {"dec": x_peer}))
+        b_out[q] = acc[q, 2 * r : 4 * r, quarter:].astype(BF)
+        rb[q] = go(remote(RB, q, b_out.at[q], b_in.at[q], {"dec": y_peer}))
+
+    def fold2(q):
+        ra[q].wait_recv()
+        a2_out[q] = (acc[q, 2 * r : 3 * r, 0:quarter] + a_in[q, r : 2 * r].astype(F32)).astype(BF)
+        ra2[q] = go(remote(RA2, q, a2_out.at[q], a2_in.at[q], {"dec": y_peer}))
+        rb[q].wait_recv()
+        b2_out[q] = (acc[q, r : 2 * r, quarter:] + b_in[q, r : 2 * r].astype(F32)).astype(BF)
+        rb2[q] = go(remote(RB2, q, b2_out.at[q], b2_in.at[q], {"dec": x_peer}))
+        acc[q, 0:r, 0:quarter] = acc[q, 0:r, 0:quarter] + a_in[q, 0:r].astype(F32)
+        acc[q, 0:r, quarter:] = acc[q, 0:r, quarter:] + b_in[q, 0:r].astype(F32)
+
+    def fold3(q):
+        ra2[q].wait_recv()
+        rb2[q].wait_recv()
+        acc[q, 0:r, 0:quarter] = acc[q, 0:r, 0:quarter] + a2_in[q].astype(F32)
+        acc[q, 0:r, quarter:] = acc[q, 0:r, quarter:] + b2_in[q].astype(F32)
+        if q:
+            z_out[q] = acc[q, 0:r].astype(BF)
+            rz[q] = go(remote(RZ, q, z_out.at[q], z_in.at[q], {"dec": z_peers[q]}))
+
+    gather_a(0)
     first = []
     for m in range(1, count):
         peer = (me + m) % count
@@ -254,95 +357,15 @@
         first.append(copy)
     mig_in[0] = out_cache[me]
 
-    def gather(q):
-        if q < 3:
-            zg[q + 1].wait_recv()
-            spread(q + 1)
-        y1[q].wait_recv()
-        x2 = go(remote(X2, q, slot(q, 2, 0, quarter), slot(q, 3, 0, quarter), {"dec": x_peer}))
-        x1[q].wait_recv()
-        y2 = go(remote(Y2, q, slot(q, 1, quarter), slot(q, 3, quarter), {"dec": y_peer}))
-        x2.wait_recv()
-        y2.wait_recv()
-        return go(remote(SIB, q, gath.at[core, q], gath.at[core, q], {"tp": 1 - core}))
-
-    def apply(q):
-        if q == 0:
-            weights[0].wait()
-            weights[1].wait()
-
-        @pl.loop(0, act.shape[1] // 256)
-        def _(i):
-            cols = pl.ds(pl.multiple_of(i * 256, 256), 256)
-
-            def product(w):
-                return jnp.dot(
-                    gath[0, q, :, 0:half], w[0:half, cols], preferred_element_type=F32
-                ) + jnp.dot(
-                    gath[1, q, :, 0:half], w[half : 2 * half, cols], preferred_element_type=F32
-                )
-
-            g = product(wg)
-            act[:, cols] = (g / (1.0 + jnp.exp(-g)) * product(wu)).astype(BF)
-
-        if q == 0:
-            weights[2].wait()
-        probs = gath[0, q, :, half:].astype(F32)
-        lanes = lax.broadcasted_iota(jnp.int32, probs.shape, 1)
-        mine = (lanes == me) | (lanes == me + 16)
-        weight = jnp.sum(jnp.where(mine, probs, 0.0), axis=-1, keepdims=True)
-        step = 512
-
-        @pl.loop(0, half // step)
-        def _(i):
-            to = pl.ds(pl.multiple_of(i * step, step), step)
-            cols = pl.ds(pl.multiple_of((1 - core) * half + i * step, step), step)
-            tp_out[q, :, to] = (
-                jnp.dot(act[...], wd[:, cols], preferred_element_type=F32) * weight
-            ).astype(BF)
-
-        copy = go(remote(TP, q, tp_out.at[q], tp_in.at[q], {"tp": 1 - core}))
-
-        @pl.loop(0, half // step)
-        def _(i):
-            to = pl.ds(pl.multiple_of(i * step, step), step)
-            cols = pl.ds(pl.multiple_of(core * half + i * step, step), step)
-            acc[q, :, to] = jnp.dot(act[...], wd[:, cols], preferred_element_type=F32) * weight
-
-        return copy
-
-    ra, rb, ra2, rb2, rz = {}, {}, {}, {}, {}
-    r = rows
-
-    def fold1(q, copy):
-        copy.wait_recv()
-        acc[q] = acc[q] + tp_in[q].astype(F32)
-        a_out[q, 0:r] = acc[q, r : 2 * r, 0:quarter].astype(BF)
-        a_out[q, r : 2 * r] = acc[q, 3 * r : 4 * r, 0:quarter].astype(BF)
-        ra[q] = go(remote(RA, q, a_out.at[q], a_in.at[q], {"dec": x_peer}))
-        b_out[q] = acc[q, 2 * r : 4 * r, quarter:].astype(BF)
-        rb[q] = go(remote(RB, q, b_out.at[q], b_in.at[q], {"dec": y_peer}))
-
-    def fold2(q):
-        ra[q].wait_recv()
-        a2_out[q] = (acc[q, 2 * r : 3 * r, 0:quarter] + a_in[q, r : 2 * r].astype(F32)).astype(BF)
-        ra2[q] = go(remote(RA2, q, a2_out.at[q], a2_in.at[q], {"dec": y_peer}))
-        rb[q].wait_recv()
-        b2_out[q] = (acc[q, r : 2 * r, quarter:] + b_in[q, r : 2 * r].astype(F32)).astype(BF)
-        rb2[q] = go(remote(RB2, q, b2_out.at[q], b2_in.at[q], {"dec": x_peer}))
-        acc[q, 0:r, 0:quarter] = acc[q, 0:r, 0:quarter] + a_in[q, 0:r].astype(F32)
-        acc[q, 0:r, quarter:] = acc[q, 0:r, quarter:] + b_in[q, 0:r].astype(F32)
-
-    def fold3(q):
-        ra2[q].wait_recv()
-        rb2[q].wait_recv()
-        acc[q, 0:r, 0:quarter] = acc[q, 0:r, 0:quarter] + a2_in[q].astype(F32)
-        acc[q, 0:r, quarter:] = acc[q, 0:r, quarter:] + b2_in[q].astype(F32)
-        if q:
-            z_out[q] = acc[q, 0:r].astype(BF)
-            rz[q] = go(remote(RZ, q, z_out.at[q], z_in.at[q], {"dec": z_peers[q]}))
-
-    sib = gather(0)
+    gather_b(0)
+    tp0 = apply(0)
+    gather_a(1)
+    fold1(0, tp0)
+    gather_b(1)
+    tp1 = apply(1)
+    gather_a(2)
+    fold1(1, tp1)
+    fold2(0)
     for copy in first:
         copy.wait()
     width = mig_out.shape[2]
@@ -366,26 +389,18 @@
         copy.start()
         second.append(copy)
 
-    sib.wait_recv()
-    tp0 = apply(0)
-    sib = gather(1)
-    fold1(0, tp0)
-    sib.wait_recv()
-    tp1 = apply(1)
-    fold2(0)
-    sib = gather(2)
-    fold1(1, tp1)
+
+    gather_b(2)
+    tp2 = apply(2)
+    gather_a(3)
+    fold1(2, tp2)
+    fold2(1)
     fold3(0)
-    sib.wait_recv()
-    tp2 = apply(2)
-    fold2(1)
-    sib = gather(3)
-    fold1(2, tp2)
-    fold3(1)
-    sib.wait_recv()
+    gather_b(3)
     tp3 = apply(3)
     fold2(2)
     fold1(3, tp3)
+    fold3(1)
     fold3(2)
     fold2(3)
     for copy in second:
@@ -421,7 +436,7 @@
         vm((4, rows, half), BF), vm((4, rows, half), BF),
         vm(out_cache.shape, BF), vm((16, PIECE, 128), BF),
         pltpu.SemaphoreType.DMA((3,)),
-        pltpu.SemaphoreType.DMA((13, 4)), pltpu.SemaphoreType.DMA((13, 4)),
+        pltpu.SemaphoreType.DMA((16, 4)), pltpu.SemaphoreType.DMA((16, 4)),
         pltpu.SemaphoreType.DMA((16,)), pltpu.SemaphoreType.DMA((16,)),
         pltpu.SemaphoreType.DMA((16,)), pltpu.SemaphoreType.DMA((16,)),
         pltpu.SemaphoreType.DMA,
@@ -567,7 +582,7 @@
             pltpu.SemaphoreType.DMA(block_table.shape),
             pltpu.SemaphoreType.DMA(block_table.shape),
         ],
-        compiler_params=pltpu.CompilerParams(vmem_limit_bytes=32 * 1024 * 1024),
+        compiler_params=pltpu.CompilerParams(vmem_limit_bytes=56 * 1024 * 1024),
     )(block_table, lengths, new_group, q, new, pool)
     moe_out, incoming = exchange(
         hidden_rows, norm_gain.astype(F32).reshape(2, -1), routes, route_logits,
@@ -576,10 +591,11 @@
     pool_after = pl.pallas_call(
         place_kernel,
         out_shape=jax.ShapeDtypeStruct(pool.shape, BF),
-        in_specs=[scalar] * 2 + [outside] * 2,
+        in_specs=[scalar] * 2 + [inside, outside],
         out_specs=outside,
         scratch_shapes=[pltpu.SemaphoreType.DMA((block_table.shape[1],))],
         input_output_aliases={3: 0},
+        compiler_params=pltpu.CompilerParams(vmem_limit_bytes=56 * 1024 * 1024),
     )(block_table, new_group, incoming, pool_now)
     back = pool_after.reshape(blocks, block_tokens, kv_width // HD, 2, HD)
     pool_after = back.transpose(0, 1, 3, 2, 4).reshape(kv_pool.shape)

time: 120 us -> 87.7 us (0.73)
  Pallas kernels: 109 us -> 82.1 us
  local copies, waits for them, and re-layouts: 8.99 us -> 4.44 us
    pallas_call x1, Pallas kernels: 88.5 us -> 70.9 us  [exchange(): pl.pallas_call(exchange_kernel, out_shape=(jax.ShapeDtypeStruct((steps, r...]
    pallas_call x1, Pallas kernels: 9.87 us -> 1.74 us  [body_slots(): pl.pallas_call(place_kernel, out_shape=jax.ShapeDtypeStruct(pool.shape, B...]
    unnamed x13 -> x1, local copies, waits for them, and re-layouts: 6.82 us -> 1.57 us
    pallas_call x1, Pallas kernels: 10.9 us -> 9.49 us  [body_slots(): pl.pallas_call(cache_kernel, out_shape=(jax.ShapeDtypeStruct(q.shape, BF)...]
where the time goes in v2:
time: 87.7 us; the launch traced here: 87.2 us
  Pallas kernels  82.1 us (94%)
  local copies, waits for them, and re-layouts  4.44 us (5%)
    pallas_call x1, Pallas kernels, exchange(): pl.pallas_call(exchange_kernel, out_shape=(jax.ShapeDtypeStruct((steps, r...  70.9 us
    pallas_call x1, Pallas kernels, body_slots(): pl.pallas_call(cache_kernel, out_shape=(jax.ShapeDtypeStruct(q.shape, BF)...  9.49 us

profile of v2, /device:TPU:0, one launch (start us, length us, event | category | flops | bytes accessed | tf_op | source)
XLA Modules:
  0.0 87.2 jit_solution(16395157753912600835)
XLA Ops:
  0.6 1.3 %reshape.49.gain = f32[2,2048]{1,0:T(2,128)} reshape(bf16[4096]{0:T(1024)(128)(2,1)} %param.20) | data formatting | bytes 24576 | tf_op jit(solution)/shard_map/reshape | solution.py:588
  1.9 0.8 reshape.51
  2.8 0.7 tile.2
  3.5 9.5 %shard_map.148 = (bf16[4,32,8,128]{3,2,1,0:T(8,128)(2,1)}, bf16[8192,128]{1,0:T(8,128)(2,1)}, bf16[16,80,128]{2,1,0:T(8,128)(2,1)}) custom-call(s32[8,8]{1,0:T(8,128)} %table.3, s32[8]{0:T(128)} %lengths.1, s32[8]{0:T(128)} %moves.3, bf16[4,32,8,128]{3,2,1,0:T(8,128)(2,1)} %bitcast.23, f32[4,8,16,128]{3,2,1,0:T(8,128)} %bitcast.22, bf16[8192,128]{1,0:T(8,128)(2,1)} %bitcast.20), custom_call_target="tpu_custom_call" | custom-call | tf_op jit(solution)/shard_map/pallas_call | solution.py:569
  13.0 70.9 %shard_map.149 = (bf16[4,8,2048]{2,1,0:T(8,128)(2,1)}, bf16[1024,128]{1,0:T(8,128)(2,1)}) custom-call(bf16[4,8,2048]{2,1,0:T(8,128)(2,1)} %hid.1, f32[2,2048]{1,0:T(2,128)} %reshape.49.gain, s32[4,8,8]{2,1,0:T(8,128)} %routes.1, f32[4,8,8]{2,1,0:T(8,128)} %logits.1, bf16[16,80,128]{2,1,0:T(8,128)(2,1)} %get-tuple-element.9.out_cache, ...), custom_call_target="tpu_custom_call" | custom-call | tf_op jit(solution)/shard_map/pallas_call | solution.py:446
  83.9 1.7 %shard_map.150 = bf16[8192,128]{1,0:T(8,128)(2,1)} custom-call(s32[8,8]{1,0:T(8,128)} %table.3, s32[8]{0:T(128)} %moves.3, bf16[1024,128]{1,0:T(8,128)(2,1)} %get-tuple-element.11.incoming, bf16[8192,128]{1,0:T(8,128)(2,1)} %get-tuple-element.12.pool), custom_call_target="tpu_custom_call", output_to_operand_aliasing={{}: (3, {})} | custom-call | tf_op jit(solution)/shard_map/pallas_call | solution.py:591
  85.7 1.6 %copy.31 = bf16[4,8,2048]{2,1,0:T(8,128)(2,1)} copy(bf16[4,8,2048]{2,1,0:T(8,128)(2,1)} %get-tuple-element.17) | data formatting | bytes 262144
  (2 shorter events, 0.0 us)
